TPU v7x, 512 devices: a whole 4x4x16 slice. The times are simulated.
512 devices in a mesh: seq: 32 (over x, z_hi, core), col: 16 (over y, z_lo).
Axes of the slice: x: 4, y: 4, z: 16 (z_hi: 4, z_lo: 4; z = z_hi * 4 + z_lo), core: 2. Of those that a mesh axis runs over, the one named last changes fastest.
Arguments:
- alignment_embedding_tensor: bfloat16 [512, 128, 768], P('seq', 'col'), may hold values from -3 to 3
- horizontal_attention_triples: bfloat16 [512, 128, 2304], P('seq', 'col'), may hold values from -10 to 10
- occupancy_indicator: int32 [512, 128], P('seq', 'col'), may hold values from 0 to 1, as said below
- horizontal_attention_exit_matrix: bfloat16 [768, 768], P('col'), may hold values from -0.21875 to 0.21875
- vertical_attention_entry_matrix: bfloat16 [768, 2304], P('col'), may hold values from -0.43164062 to 0.43164062
- vertical_attention_exit_matrix: bfloat16 [768, 768], P('col'), may hold values from -0.21875 to 0.21875
- vertical_layernorm_scaling: float32 [768], replicated, may hold values from 0.25 to 1.75
Outputs:
- mixed: float32 [512, 128, 768], P('seq', 'col')
Inputs may be any that keep to these rules, and one draw needn't show every extreme that they name: `occupancy_indicator`: every column holds a residue in some sequence.
All inputs are finite; a program needn't handle non-finite values.
Results may differ from a plain program's by a relative error of at most 0.035.
Values may be sent and summed in bfloat16 or wider, within the bound.
A program may use at most 64 MiB of HBM per device.

v0:
```python
import math
import jax
import jax.numpy as jnp
from jax import lax
from jax.sharding import Mesh
from jax.sharding import PartitionSpec as P

H = 12
DH = 64
COL = ("col_0", "col_1")


def in_one_piece(arrays, axis, dim, along):
    ends, at = ([], 0)
    for a in arrays[:-1]:
        at += a.shape[along]
        ends.append(at)
    both = jnp.concatenate(arrays, axis=along)
    return tuple(jnp.split(lax.all_gather(both, axis, axis=dim, tiled=True), ends, axis=along))


def from_everyone(array, axis):
    length = lax.axis_size(axis)
    return lax.all_to_all(
        jnp.broadcast_to(array[None], (length, *array.shape)), axis, 0, 0, tiled=True
    )


def of_everyone(array, axis):
    return from_everyone(array, axis).sum(axis=0)


def whole_of(array, axes, dim):
    filled = array
    for number in range(len(axes) - 1, -1, -1):
        filled = lax.all_gather(filled, axes[number], axis=dim, tiled=True)
    return filled


def items_in_groups(array, axis, split_dim, concat_dim, work, item_dim, out_dim):
    items = jax.tree.leaves(array)[0].shape[item_dim]
    count = 2 if items % 2 == 0 else 1
    gathered = []
    for k in range(count):
        group = jax.tree.map(
            lambda a: lax.slice_in_dim(
                a, k * (items // count), (k + 1) * (items // count), axis=item_dim
            ),
            array,
        )
        gathered.append(
            work(
                lax.all_to_all(
                    group, axis, split_axis=split_dim, concat_axis=concat_dim, tiled=True
                )
            )
        )
    return jax.tree.map(lambda *parts: jnp.concatenate(parts, axis=out_dim), *gathered)


def attend_columns(pieces):
    block, keep = pieces
    cq = block[..., :DH]
    ck = block[..., DH : 2 * DH]
    cv = block[..., 2 * DH :]
    scores = jnp.einsum("rgud,sgud->gurs", cq, ck, preferred_element_type=jnp.float32) / math.sqrt(
        DH
    )
    mask_keys = jnp.transpose(keep, (1, 2, 0))[:, :, None, :]
    scores = jnp.where(mask_keys > 0, scores, -1000000000.0)
    probs = jax.nn.softmax(scores, axis=-1).astype(jnp.bfloat16)
    return jnp.einsum("gurs,sgud->rgud", probs, cv, preferred_element_type=jnp.float32).astype(
        jnp.bfloat16
    )


def per_device(
    alignment_embedding_tensor,
    horizontal_attention_triples,
    occupancy_indicator,
    horizontal_attention_exit_matrix,
    vertical_attention_entry_matrix,
    vertical_attention_exit_matrix,
    vertical_layernorm_scaling,
):
    protein_extent, site_extent, embedding_dimension = alignment_embedding_tensor.shape
    total_rows = protein_extent * lax.axis_size("seq")
    live = occupancy_indicator.astype(jnp.bfloat16)
    parts = horizontal_attention_triples.reshape(protein_extent, site_extent, 3, H, DH)
    query = parts[:, :, 0] * live[:, :, None, None]
    keys = parts[:, :, 1]
    values = parts[:, :, 2]
    scale = 1.0 / (math.sqrt(DH) * math.sqrt(total_rows))
    full_wo_row, full_qkv, full_wo_col = in_one_piece(
        (
            horizontal_attention_exit_matrix,
            vertical_attention_entry_matrix,
            vertical_attention_exit_matrix,
        ),
        COL,
        0,
        1,
    )
    all_keys = lax.all_gather(keys, COL, axis=1, tiled=True)
    partial_value = (
        jnp.einsum("rihd,rjhd->hij", query, all_keys, preferred_element_type=jnp.float32) * scale
    )
    logits = of_everyone(partial_value, "seq")
    all_values = whole_of(values, COL, 1)
    row_probs = jax.nn.softmax(logits, axis=-1).astype(jnp.bfloat16)
    context = jnp.einsum(
        "hij,rjhd->rihd", row_probs, all_values, preferred_element_type=jnp.float32
    ).astype(jnp.bfloat16)
    merged_attended_heads = context.reshape(protein_extent * site_extent, embedding_dimension)
    skip_connection_hidden = alignment_embedding_tensor.reshape(
        protein_extent * site_extent, embedding_dimension
    ).astype(jnp.float32) + jnp.dot(
        merged_attended_heads, full_wo_row, preferred_element_type=jnp.float32
    )
    center = skip_connection_hidden - jnp.mean(skip_connection_hidden, axis=-1, keepdims=True)
    variance = jnp.mean(center * center, axis=-1, keepdims=True)
    normed = (center * lax.rsqrt(variance + 1e-05) * vertical_layernorm_scaling).astype(
        jnp.bfloat16
    )
    col_qkv = jnp.dot(normed, full_qkv, preferred_element_type=jnp.float32).astype(jnp.bfloat16)
    seq_count = lax.axis_size("seq")
    units = site_extent * H // seq_count
    col_qkv = jnp.transpose(col_qkv.reshape(protein_extent, site_extent, 3, H, DH), (0, 1, 3, 2, 4))
    col_qkv = col_qkv.reshape(protein_extent, seq_count, units, 3 * DH)
    live_units = jnp.broadcast_to(live[:, :, None], (protein_extent, site_extent, H)).reshape(
        protein_extent, seq_count, units
    )
    attended = items_in_groups((col_qkv, live_units), "seq", 1, 0, attend_columns, 2, 2)
    returned_cols = lax.all_to_all(attended, "seq", split_axis=0, concat_axis=1, tiled=True)
    col_context = returned_cols.reshape(protein_extent * site_extent, embedding_dimension)
    mixed = skip_connection_hidden + jnp.dot(
        col_context, full_wo_col, preferred_element_type=jnp.float32
    )
    return mixed.reshape(protein_extent, site_extent, embedding_dimension)


def solution(mesh):
    torus = Mesh(mesh.devices.reshape(mesh.shape["seq"], 4, 4), ("seq", "col_0", "col_1"))
    in_specs = (
        P("seq", COL, None),
        P("seq", COL, None),
        P("seq", COL),
        P(COL, None),
        P(COL, None),
        P(COL, None),
        P(),
    )
    out_specs = P("seq", COL, None)
    return jax.shard_map(
        per_device, mesh=torus, in_specs=in_specs, out_specs=out_specs, check_vma=False
    )
```

profile of v0, /device:TPU:1, one launch (start us, length us, event | category | flops | bytes accessed | tf_op | source)
XLA Modules:
  0.0 497.0 jit_solution(10762542921084627330)
XLA Ops:
  6.5 1.9 reshape.85
  8.5 0.3 fusion.40
  8.8 1.0 copy.42
  9.9 0.3 copy.45
  10.2 37.4 %all-gather.1 = bf16[16,32,1,12,64]{4,0,3,2,1:T(8,128)(2,1)} all-gather(bf16[16,8,1,12,64]{4,0,3,2,1:T(8,128)(2,1)S(1)} %copy.45), channel_id=3, replica_groups=mesh['seq'=32,'col_0'=4,'col_1'=4] {'col_1'}, dimensions={1}, use_global_device_ids=true | all-gather | bytes 983040 | tf_op jit(solution)/shard_map/all_gather | solution.py:36
  47.5 0.0 all-gather.7.cloned.1.call-start
  47.6 0.8 pad_maximum_fusion
  48.5 0.1 copy.41
  48.5 1.0 fusion.31
  49.6 124.1 %all-gather.9.cloned.1.call-done = bf16[16,128,1,12,64]{4,0,3,2,1:T(8,128)(2,1)} async-done(((bf16[16,8,1,12,64]{4,0,3,2,1:T(8,128)(2,1)}), bf16[16,128,1,12,64]{4,0,3,2,1:T(8,128)(2,1)}) %all-gather.9.cloned.1.call-update) | async-done | bytes 3145744 | tf_op jit(solution)/shard_map/all_gather | solution.py:104
  173.6 7.9 %copy.43 = bf16[16,128,1,12,64]{1,4,0,3,2:T(8,128)(2,1)S(1)} copy(bf16[16,128,1,12,64]{4,0,3,2,1:T(8,128)(2,1)} %all-gather.9.cloned.1.call-done) | data formatting | bytes 6291456 | tf_op jit(solution)/shard_map/all_gather | solution.py:104
  181.6 1.6 fusion.28
  183.2 1.4 broadcast_in_dim.16
  184.6 17.1 %all-to-all-start = ((f32[32,12,8,128]{3,2,1,0:T(8,128)}), f32[32,12,8,128]{3,2,1,0:T(8,128)}, u32[]{:S(2)}, u32[]{:S(2)}) async-start(f32[32,12,8,128]{3,2,1,0:T(8,128)} %broadcast_in_dim.16), calls=%async_computation | async-start | bytes 3145728 | tf_op jit(solution)/shard_map/all_to_all | solution.py:24
  201.8 48.3 %all-gather.11.cloned.1.call-done = bf16[16,128,1,12,64]{4,0,3,2,1:T(8,128)(2,1)} async-done(((bf16[16,32,1,12,64]{4,0,3,2,1:T(8,128)(2,1)}), bf16[16,128,1,12,64]{4,0,3,2,1:T(8,128)(2,1)}) %all-gather.11.cloned.1.call-update) | async-done | bytes 3145744 | tf_op jit(solution)/shard_map/all_gather | solution.py:36
  250.1 7.9 %copy.46 = bf16[16,128,1,12,64]{1,4,0,3,2:T(8,128)(2,1)S(1)} copy(bf16[16,128,1,12,64]{4,0,3,2,1:T(8,128)(2,1)} %all-gather.11.cloned.1.call-done) | data formatting | bytes 6291456 | tf_op jit(solution)/shard_map/all_gather | solution.py:36
  258.0 19.1 %all-to-all-done = f32[32,12,8,128]{3,2,1,0:T(8,128)} async-done(((f32[32,12,8,128]{3,2,1,0:T(8,128)}), f32[32,12,8,128]{3,2,1,0:T(8,128)}, u32[]{:S(2)}, u32[]{:S(2)}) %all-to-all-start) | async-done | bytes 1572896 | tf_op jit(solution)/shard_map/all_to_all | solution.py:24
  277.2 0.6 broadcast_in_dim.23
  277.8 7.0 %all-to-all-start.2 = ((bf16[16,32,3]{0,2,1:T(4,128)(2,1)}), bf16[16,32,3]{0,2,1:T(4,128)(2,1)}, u32[]{:S(2)}, u32[]{:S(2)}) async-start(bf16[16,32,3]{0,2,1:T(4,128)(2,1)} %broadcast_in_dim.23), calls=%async_computation.2 | async-start | bytes 65536 | tf_op jit(solution)/shard_map/all_to_all | solution.py:53
  284.9 1.5 reduce_sum.45
  286.4 0.6 copy-done
  287.0 0.2 fusion.41
  287.2 3.4 fusion.16
  290.6 0.3 copy.47
  290.9 0.3 reshape.86
  291.2 104.0 %all-gather.7.cloned.1.call-done = bf16[768,3840]{1,0:T(8,128)(2,1)} async-done(((bf16[48,3840]{1,0:T(8,128)(2,1)}), bf16[768,3840]{1,0:T(8,128)(2,1)}) %all-gather.7.cloned.1.call-update) | async-done | bytes 5898256 | tf_op jit(solution)/shard_map/all_gather | solution.py:19
  395.2 1.7 fusion.42
  396.9 0.2 multiply_reduce_fusion
  397.1 2.7 convolution_convert_fusion
  399.8 1.0 reshape.87
  400.8 0.8 copy.48
  401.7 2.0 reshape.88
  403.7 13.0 %all-to-all-start.1 = ((bf16[16,32,3,192]{3,0,2,1:T(8,128)(2,1)}), bf16[16,32,3,192]{3,0,2,1:T(8,128)(2,1)S(1)}, u32[]{:S(2)}, u32[]{:S(2)}) async-start(bf16[16,32,3,192]{3,0,2,1:T(8,128)(2,1)} %reshape.88), calls=%async_computation.1 | async-start | bytes 1572864 | tf_op jit(solution)/shard_map/all_to_all | solution.py:53
  416.7 0.8 compare_bitcast_fusion
  417.5 0.1 gt.26
  417.6 41.3 %all-to-all-done.1 = bf16[16,32,3,192]{3,0,2,1:T(8,128)(2,1)S(1)} async-done(((bf16[16,32,3,192]{3,0,2,1:T(8,128)(2,1)}), bf16[16,32,3,192]{3,0,2,1:T(8,128)(2,1)S(1)}, u32[]{:S(2)}, u32[]{:S(2)}) %all-to-all-start.1) | async-done | bytes 589856 | tf_op jit(solution)/shard_map/all_to_all | solution.py:53
  458.9 0.1 copy.49
  459.0 0.6 fusion.32
  459.6 1.3 fusion.43
  460.9 0.5 fusion.22
  461.3 0.3 copy.55
  461.7 0.4 reshape.102
  462.0 25.0 %all_to_all.50 = bf16[32,2,1536]{2,1,0:T(2,128)(2,1)S(1)} all-to-all(bf16[32,2,1536]{2,1,0:T(2,128)(2,1)S(1)} %reshape.102), channel_id=1, replica_groups=mesh['seq'=32,'col_0'=4,'col_1'=4] {'seq'}, dimensions={0} | all-to-all | bytes 393216 | tf_op jit(solution)/shard_map/all_to_all | solution.py:134
  487.1 0.3 reshape.103
  487.4 0.1 copy.56
  487.4 0.3 copy.57
  487.8 0.4 reshape.92
  488.1 2.3 fusion.15
  (22 shorter events, 0.2 us)
Async XLA Ops:
  6.5 167.1 %all-gather.9.cloned.1.call-start = ((), (), s32[]{:S(2)}) async-start(), calls=%async_computation.5 | async-start | bytes 6684672 | tf_op jit(solution)/shard_map/all_gather | solution.py:104
  8.8 38.8 %copy-start.1 = (bf16[48,2304]{1,0:T(8,128)(2,1)S(1)}, bf16[48,2304]{1,0:T(8,128)(2,1)}, u32[]{:S(2)}) copy-start(bf16[48,2304]{1,0:T(8,128)(2,1)} %param.11) | copy-start | bytes 663556
  8.8 38.8 %copy-start.2 = (bf16[48,768]{1,0:T(8,128)(2,1)S(1)}, bf16[48,768]{1,0:T(8,128)(2,1)}, u32[]{:S(2)}) copy-start(bf16[48,768]{1,0:T(8,128)(2,1)} %param.12) | copy-start | bytes 221188
  8.8 38.8 %copy-start.3 = (bf16[48,768]{1,0:T(8,128)(2,1)S(1)}, bf16[48,768]{1,0:T(8,128)(2,1)}, u32[]{:S(2)}) copy-start(bf16[48,768]{1,0:T(8,128)(2,1)} %param.10) | copy-start | bytes 221188
  9.8 38.6 %copy-start.4 = (s32[16,8]{0,1:T(8,128)S(1)}, s32[16,8]{0,1:T(8,128)}, u32[]{:S(2)}) copy-start(s32[16,8]{0,1:T(8,128)} %param.9) | copy-start | bytes 1540
  9.8 240.2 %all-gather.11.cloned.1.call-start = ((), (), s32[]{:S(2)}) async-start(), calls=%async_computation.6 | async-start | bytes 7864320 | tf_op jit(solution)/shard_map/all_gather | solution.py:36
  47.5 347.7 %all-gather.7.cloned.1.call-start = ((), (), s32[]{:S(2)}) async-start(), calls=%async_computation.4 | async-start | bytes 6266880 | tf_op jit(solution)/shard_map/all_gather | solution.py:19
  184.6 92.6 %all-to-all-start = ((f32[32,12,8,128]{3,2,1,0:T(8,128)}), f32[32,12,8,128]{3,2,1,0:T(8,128)}, u32[]{:S(2)}, u32[]{:S(2)}) async-start(f32[32,12,8,128]{3,2,1,0:T(8,128)} %broadcast_in_dim.16), calls=%async_computation | async-start | bytes 3145728 | tf_op jit(solution)/shard_map/all_to_all | solution.py:24
  277.8 125.9 %all-to-all-start.2 = ((bf16[16,32,3]{0,2,1:T(4,128)(2,1)}), bf16[16,32,3]{0,2,1:T(4,128)(2,1)}, u32[]{:S(2)}, u32[]{:S(2)}) async-start(bf16[16,32,3]{0,2,1:T(4,128)(2,1)} %broadcast_in_dim.23), calls=%async_computation.2 | async-start | bytes 65536 | tf_op jit(solution)/shard_map/all_to_all | solution.py:53
  286.4 0.6 copy-start
  287.2 110.0 %copy-start.5 = (f32[768]{0:T(1024)S(1)}, f32[768]{0:T(1024)}, u32[]{:S(2)}) copy-start(f32[768]{0:T(1024)} %param.13) | copy-start | bytes 9220
  403.7 55.2 %all-to-all-start.1 = ((bf16[16,32,3,192]{3,0,2,1:T(8,128)(2,1)}), bf16[16,32,3,192]{3,0,2,1:T(8,128)(2,1)S(1)}, u32[]{:S(2)}, u32[]{:S(2)}) async-start(bf16[16,32,3,192]{3,0,2,1:T(8,128)(2,1)} %reshape.88), calls=%async_computation.1 | async-start | bytes 1572864 | tf_op jit(solution)/shard_map/all_to_all | solution.py:53
Sparse Core Ops, SparseCore 0:
  10.0 163.6 all-gather.8
  175.7 74.3 all-gather.10
  252.2 142.9 all-gather.6
where the time goes:
time: 498 us; the launch traced here: 497 us
  waiting for transfers between devices  337 us (68%)
  blocking collectives  62.4 us (13%)
  starting transfers between devices  37.2 us (7%)
  local copies, waits for them, and re-layouts  28.5 us (6%)
  between operations  13.4 us (3%)
  matrix products  12.8 us (3%)
  other arithmetic  5.73 us (1%)
    all_gather x1, waiting for transfers between devices, per_device(): all_keys = lax.all_gather(keys, COL, axis=1, tiled=True)  124 us
    all_gather x1, waiting for transfers between devices, in_one_piece(): lax.all_gather(both, axis, axis=dim, tiled=True)  104 us
    all_gather x1, waiting for transfers between devices, whole_of(): filled = lax.all_gather(filled, axes[number], axis=dim, tiled=True)  48.3 us
    all_to_all x2, waiting for transfers between devices, items_in_groups(): lax.all_to_all(group, axis, split_axis=split_dim, concat_axis=concat_dim,...  41.3 us
    all_gather x1, blocking collectives, whole_of(): filled = lax.all_gather(filled, axes[number], axis=dim, tiled=True)  37.4 us
    all_to_all x1, blocking collectives, per_device(): lax.all_to_all(attended, 'seq', split_axis=0, concat_axis=1, tiled=True)  25 us
    all_to_all x2, starting transfers between devices, items_in_groups(): lax.all_to_all(group, axis, split_axis=split_dim, concat_axis=concat_dim,...  20 us
    all_to_all x1, waiting for transfers between devices, from_everyone(): lax.all_to_all(jnp.broadcast_to(array[None], (length, *array.shape)), axi...  19.1 us
  transfers between devices with their start and end apart: 6, of which 5 were waited for; matrix products, arithmetic and copies ran while one was open for 7% of the time, Pallas kernels for 0%

commit v1 on v0

--- a/solution.py
+++ b/solution.py
@@ -101,7 +101,9 @@
         0,
         1,
     )
-    all_keys = lax.all_gather(keys, COL, axis=1, tiled=True)
+    all_keys = jnp.concatenate(
+        lax.all_to_all(jnp.stack([keys] * lax.axis_size(COL)), COL, 0, 0), axis=1
+    )
     partial_value = (
         jnp.einsum("rihd,rjhd->hij", query, all_keys, preferred_element_type=jnp.float32) * scale
     )

time: 498 us -> 464 us (0.932)
  waiting for transfers between devices: 337 us -> 216 us
  blocking collectives: 62.4 us -> 116 us
  local copies, waits for them, and re-layouts: 28.5 us -> 47.2 us
  starting transfers between devices: 37.2 us -> 46.7 us
    all_gather x1 -> x0, waiting for transfers between devices: 124 us -> none  [per_device(): all_keys = lax.all_gather(keys, COL, axis=1, tiled=True)]
    all_gather x1, blocking collectives: 37.4 us -> 92.6 us  [whole_of(): filled = lax.all_gather(filled, axes[number], axis=dim, tiled=True)]
    unnamed x14 -> x19, local copies, waits for them, and re-layouts: 1.31 us -> 26.7 us
    all_to_all x0 -> x1, starting transfers between devices: none -> 9.19 us  [per_device(): lax.all_to_all(jnp.stack([keys] * lax.axis_size(COL)), COL, 0, 0)]
    all_gather x1 -> x0, local copies, waits for them, and re-layouts: 7.95 us -> none  [per_device(): all_keys = lax.all_gather(keys, COL, axis=1, tiled=True)]
    all_gather x1, waiting for transfers between devices: 48.3 us -> 42.1 us  [whole_of(): filled = lax.all_gather(filled, axes[number], axis=dim, tiled=True)]
    all_to_all x1, waiting for transfers between devices: 19.1 us -> 24.2 us  [from_everyone(): lax.all_to_all(jnp.broadcast_to(array[None], (length, *array.shape)), axi...]
  transfers between devices with their start and end apart: 6 -> 6, of which waited for: 5 -> 4; matrix products, arithmetic and copies ran while one was open for 7% -> 9% of each run, Pallas kernels for 0% -> 0%
where the time goes in v1:
time: 464 us; the launch traced here: 462 us
  waiting for transfers between devices  216 us (47%)
  blocking collectives  116 us (25%)
  local copies, waits for them, and re-layouts  47.2 us (10%)
  starting transfers between devices  46.7 us (10%)
  matrix products  15.9 us (3%)
  between operations  13.7 us (3%)
  other arithmetic  6.78 us (1%)
    all_gather x1, waiting for transfers between devices, in_one_piece(): lax.all_gather(both, axis, axis=dim, tiled=True)  108 us
    all_gather x1, blocking collectives, whole_of(): filled = lax.all_gather(filled, axes[number], axis=dim, tiled=True)  92.6 us
    all_gather x1, waiting for transfers between devices, whole_of(): filled = lax.all_gather(filled, axes[number], axis=dim, tiled=True)  42.1 us
    all_to_all x2, waiting for transfers between devices, items_in_groups(): lax.all_to_all(group, axis, split_axis=split_dim, concat_axis=concat_dim,...  41.1 us
    unnamed x19, local copies, waits for them, and re-layouts  26.7 us
    all_to_all x1, waiting for transfers between devices, from_everyone(): lax.all_to_all(jnp.broadcast_to(array[None], (length, *array.shape)), axi...  24.2 us
    all_to_all x1, blocking collectives, per_device(): lax.all_to_all(attended, 'seq', split_axis=0, concat_axis=1, tiled=True)  23.3 us
    all_to_all x2, starting transfers between devices, items_in_groups(): lax.all_to_all(group, axis, split_axis=split_dim, concat_axis=concat_dim,...  19.5 us
  transfers between devices with their start and end apart: 6, of which 4 were waited for; matrix products, arithmetic and copies ran while one was open for 9% of the time, Pallas kernels for 0%

profile of v1, /device:TPU:1, one launch (start us, length us, event | category | flops | bytes accessed | tf_op | source)
XLA Modules:
  0.0 462.0 jit_solution(2045899409807345015)
XLA Ops:
  6.5 1.9 reshape.93
  8.5 1.3 slice_bitcast_fusion
  9.8 0.1 copy.44
  9.9 3.9 broadcast_bitcast_fusion
  13.8 12.7 %reshape.111 = bf16[16,2,49152]{2,1,0:T(2,128)(2,1)} reshape(bf16[16,16,12,8,64]{4,3,2,1,0:T(8,128)(2,1)} %broadcast_bitcast_fusion) | data formatting | bytes 6291456
  26.5 9.2 %all-to-all-start = ((bf16[16,2,49152]{2,1,0:T(2,128)(2,1)}), bf16[16,2,49152]{2,1,0:T(2,128)(2,1)S(1)}, u32[]{:S(2)}, u32[]{:S(2)}) async-start(bf16[16,2,49152]{2,1,0:T(2,128)(2,1)} %reshape.111), calls=%async_computation | async-start | bytes 6291456 | tf_op jit(solution)/shard_map/all_to_all | solution.py:105
  35.8 1.4 copy.48
  37.2 92.6 %all-gather = bf16[16,32,1,12,64]{4,0,3,2,1:T(8,128)(2,1)} all-gather(bf16[16,8,1,12,64]{4,0,3,2,1:T(8,128)(2,1)S(1)} %copy.48), channel_id=2, replica_groups=mesh['seq'=32,'col_0'=4,'col_1'=4] {'col_1'}, dimensions={1}, use_global_device_ids=true | all-gather | bytes 983040 | tf_op jit(solution)/shard_map/all_gather | solution.py:36
  129.9 0.8 pad_maximum_fusion
  130.7 0.1 copy.43
  130.8 2.1 fusion.31
  132.9 8.8 %reshape.112 = bf16[16,16,12,8,64]{4,3,2,1,0:T(8,128)(2,1)} reshape(bf16[16,2,49152]{2,1,0:T(2,128)(2,1)S(1)} %all-to-all-done) | data formatting | bytes 6291456
  141.7 4.7 %fusion.28 = f32[12,8,128]{2,1,0:T(8,128)S(1)} fusion(bf16[16,8,12,64]{3,2,1,0:T(8,128)(2,1)} %fusion.31, bf16[16,16,12,8,64]{4,3,2,1,0:T(8,128)(2,1)} %reshape.112), kind=kOutput, calls=%fused_computation.29 | convolution fusion | flops 25178112 | bytes 3391488 | tf_op jit(solution)/shard_map/rihd,rjhd->hij/dot_general | solution.py:108
  146.3 1.4 broadcast_in_dim.16
  147.8 17.9 %all-to-all-start.1 = ((f32[32,12,8,128]{3,2,1,0:T(8,128)}), f32[32,12,8,128]{3,2,1,0:T(8,128)}, u32[]{:S(2)}, u32[]{:S(2)}) async-start(f32[32,12,8,128]{3,2,1,0:T(8,128)} %broadcast_in_dim.16), calls=%async_computation.1 | async-start | bytes 3145728 | tf_op jit(solution)/shard_map/all_to_all | solution.py:24
  165.6 42.1 %all-gather.7.cloned.1.call-done = bf16[16,128,1,12,64]{4,0,3,2,1:T(8,128)(2,1)} async-done(((bf16[16,32,1,12,64]{4,0,3,2,1:T(8,128)(2,1)}), bf16[16,128,1,12,64]{4,0,3,2,1:T(8,128)(2,1)}) %all-gather.7.cloned.1.call-update) | async-done | bytes 3145744 | tf_op jit(solution)/shard_map/all_gather | solution.py:36
  207.8 7.9 %copy.49 = bf16[16,128,1,12,64]{1,4,0,3,2:T(8,128)(2,1)S(1)} copy(bf16[16,128,1,12,64]{4,0,3,2,1:T(8,128)(2,1)} %all-gather.7.cloned.1.call-done) | data formatting | bytes 6291456 | tf_op jit(solution)/shard_map/all_gather | solution.py:36
  215.7 24.2 %all-to-all-done.1 = f32[32,12,8,128]{3,2,1,0:T(8,128)} async-done(((f32[32,12,8,128]{3,2,1,0:T(8,128)}), f32[32,12,8,128]{3,2,1,0:T(8,128)}, u32[]{:S(2)}, u32[]{:S(2)}) %all-to-all-start.1) | async-done | bytes 1572896 | tf_op jit(solution)/shard_map/all_to_all | solution.py:24
  239.9 0.6 broadcast_in_dim.23
  240.5 9.6 %all-to-all-start.3 = ((bf16[16,32,3]{0,2,1:T(4,128)(2,1)}), bf16[16,32,3]{0,2,1:T(4,128)(2,1)}, u32[]{:S(2)}, u32[]{:S(2)}) async-start(bf16[16,32,3]{0,2,1:T(4,128)(2,1)} %broadcast_in_dim.23), calls=%async_computation.3 | async-start | bytes 65536 | tf_op jit(solution)/shard_map/all_to_all | solution.py:53
  250.2 1.5 reduce_sum.45
  251.7 0.6 copy-done.1
  252.3 0.2 fusion.40
  252.5 3.4 fusion.16
  255.9 0.3 copy.50
  256.2 0.3 reshape.96
  256.5 108.4 %all-gather.5.cloned.1.call-done = bf16[768,3840]{1,0:T(8,128)(2,1)} async-done(((bf16[48,3840]{1,0:T(8,128)(2,1)}), bf16[768,3840]{1,0:T(8,128)(2,1)}) %all-gather.5.cloned.1.call-update) | async-done | bytes 5898256 | tf_op jit(solution)/shard_map/all_gather | solution.py:19
  365.0 1.7 fusion.41
  366.7 0.2 multiply_reduce_fusion
  366.9 2.7 convolution_convert_fusion
  369.6 1.0 reshape.97
  370.6 0.8 copy.51
  371.4 2.0 reshape.98
  373.5 9.9 %all-to-all-start.2 = ((bf16[16,32,3,192]{3,0,2,1:T(8,128)(2,1)}), bf16[16,32,3,192]{3,0,2,1:T(8,128)(2,1)S(1)}, u32[]{:S(2)}, u32[]{:S(2)}) async-start(bf16[16,32,3,192]{3,0,2,1:T(8,128)(2,1)} %reshape.98), calls=%async_computation.2 | async-start | bytes 1572864 | tf_op jit(solution)/shard_map/all_to_all | solution.py:53
  383.4 0.8 compare_bitcast_fusion
  384.2 0.1 gt.26
  384.3 41.1 %all-to-all-done.2 = bf16[16,32,3,192]{3,0,2,1:T(8,128)(2,1)S(1)} async-done(((bf16[16,32,3,192]{3,0,2,1:T(8,128)(2,1)}), bf16[16,32,3,192]{3,0,2,1:T(8,128)(2,1)S(1)}, u32[]{:S(2)}, u32[]{:S(2)}) %all-to-all-start.2) | async-done | bytes 589856 | tf_op jit(solution)/shard_map/all_to_all | solution.py:53
  425.5 0.6 fusion.32
  426.1 1.3 fusion.42
  427.4 0.5 fusion.22
  427.8 0.3 copy.58
  428.1 0.4 reshape.113
  428.5 23.3 %all_to_all.55 = bf16[32,2,1536]{2,1,0:T(2,128)(2,1)S(1)} all-to-all(bf16[32,2,1536]{2,1,0:T(2,128)(2,1)S(1)} %reshape.113), channel_id=1, replica_groups=mesh['seq'=32,'col_0'=4,'col_1'=4] {'seq'}, dimensions={0} | all-to-all | bytes 393216 | tf_op jit(solution)/shard_map/all_to_all | solution.py:136
  451.8 0.3 reshape.114
  452.1 0.1 copy.59
  452.1 0.3 copy.60
  452.5 0.4 reshape.102
  452.9 2.3 fusion.15
  (25 shorter events, 0.2 us)
Async XLA Ops:
  8.5 5.3 %copy-start = (bf16[16,8,3,12,64]{4,3,2,1,0:T(8,128)(2,1)}, bf16[16,8,3,12,64]{4,3,2,1,0:T(8,128)(2,1)S(1)}, u32[]{:S(2)}) copy-start(bf16[16,8,3,12,64]{4,3,2,1,0:T(8,128)(2,1)S(1)} %reshape.93) | copy-start | bytes 1769476
  26.5 106.4 %all-to-all-start = ((bf16[16,2,49152]{2,1,0:T(2,128)(2,1)}), bf16[16,2,49152]{2,1,0:T(2,128)(2,1)S(1)}, u32[]{:S(2)}, u32[]{:S(2)}) async-start(bf16[16,2,49152]{2,1,0:T(2,128)(2,1)} %reshape.111), calls=%async_computation | async-start | bytes 6291456 | tf_op jit(solution)/shard_map/all_to_all | solution.py:105
  35.7 94.2 %copy-start.2 = (bf16[48,2304]{1,0:T(8,128)(2,1)S(1)}, bf16[48,2304]{1,0:T(8,128)(2,1)}, u32[]{:S(2)}) copy-start(bf16[48,2304]{1,0:T(8,128)(2,1)} %param.11) | copy-start | bytes 663556
  35.7 94.2 %copy-start.3 = (bf16[48,768]{1,0:T(8,128)(2,1)S(1)}, bf16[48,768]{1,0:T(8,128)(2,1)}, u32[]{:S(2)}) copy-start(bf16[48,768]{1,0:T(8,128)(2,1)} %param.12) | copy-start | bytes 221188
  35.7 94.2 %copy-start.4 = (bf16[48,768]{1,0:T(8,128)(2,1)S(1)}, bf16[48,768]{1,0:T(8,128)(2,1)}, u32[]{:S(2)}) copy-start(bf16[48,768]{1,0:T(8,128)(2,1)} %param.10) | copy-start | bytes 221188
  35.7 95.0 %copy-start.5 = (s32[16,8]{0,1:T(8,128)S(1)}, s32[16,8]{0,1:T(8,128)}, u32[]{:S(2)}) copy-start(s32[16,8]{0,1:T(8,128)} %param.9) | copy-start | bytes 1540
  35.7 172.1 %all-gather.7.cloned.1.call-start = ((), (), s32[]{:S(2)}) async-start(), calls=%async_computation.6 | async-start | bytes 7864320 | tf_op jit(solution)/shard_map/all_gather | solution.py:36
  129.8 235.1 %all-gather.5.cloned.1.call-start = ((), (), s32[]{:S(2)}) async-start(), calls=%async_computation.5 | async-start | bytes 6266880 | tf_op jit(solution)/shard_map/all_gather | solution.py:19
  147.8 92.2 %all-to-all-start.1 = ((f32[32,12,8,128]{3,2,1,0:T(8,128)}), f32[32,12,8,128]{3,2,1,0:T(8,128)}, u32[]{:S(2)}, u32[]{:S(2)}) async-start(f32[32,12,8,128]{3,2,1,0:T(8,128)} %broadcast_in_dim.16), calls=%async_computation.1 | async-start | bytes 3145728 | tf_op jit(solution)/shard_map/all_to_all | solution.py:24
  240.5 132.9 %all-to-all-start.3 = ((bf16[16,32,3]{0,2,1:T(4,128)(2,1)}), bf16[16,32,3]{0,2,1:T(4,128)(2,1)}, u32[]{:S(2)}, u32[]{:S(2)}) async-start(bf16[16,32,3]{0,2,1:T(4,128)(2,1)} %broadcast_in_dim.23), calls=%async_computation.3 | async-start | bytes 65536 | tf_op jit(solution)/shard_map/all_to_all | solution.py:53
  251.7 0.6 copy-start.1
  252.5 114.4 %copy-start.6 = (f32[768]{0:T(1024)S(1)}, f32[768]{0:T(1024)}, u32[]{:S(2)}) copy-start(f32[768]{0:T(1024)} %param.13) | copy-start | bytes 9220
  373.5 51.9 %all-to-all-start.2 = ((bf16[16,32,3,192]{3,0,2,1:T(8,128)(2,1)}), bf16[16,32,3,192]{3,0,2,1:T(8,128)(2,1)S(1)}, u32[]{:S(2)}, u32[]{:S(2)}) async-start(bf16[16,32,3,192]{3,0,2,1:T(8,128)(2,1)} %reshape.98), calls=%async_computation.2 | async-start | bytes 1572864 | tf_op jit(solution)/shard_map/all_to_all | solution.py:53
Sparse Core Ops, SparseCore 0:
  130.0 77.7 all-gather.6
  209.9 155.0 all-gather.4
